TPU v7x, 256 devices: a whole 4x4x8 slice. The times are simulated.
256 devices in a mesh: sec: 16 (over z, core), op: 16 (over x, y).
Axes of the slice: x: 4, y: 4, z: 8, core: 2. Of those that a mesh axis runs over, the one named last changes fastest.
Arguments:
- theta: float32 [32, 512, 512], P('sec', 'op'), may hold values from -6 to 6
- counts: int32 [32], P('sec'), may hold values from 256 to 512, as said below
- pair_source: int32 [256], P('sec'), may hold values from 0 to 1
- pair_target: int32 [256], P('sec'), may hold values from 0 to 31
- left_ops: float32 [1024, 512, 512], P(('sec', 'op')), may hold values from -0.25 to 0.25
- right_ops: float32 [1024, 512, 512], P(('sec', 'op')), may hold values from -0.25 to 0.25
Outputs:
- cheb_last: float32 [32, 512, 512], P('sec', 'op')
- cheb_prev: float32 [32, 512, 512], P('sec', 'op')
Inputs may be any that keep to these rules, and one draw needn't show every extreme that they name: `counts`: every sector has between 256 and 512 live states; some sector has exactly 512 and some exactly 256.
All inputs are finite; a program needn't handle non-finite values.
Results may differ from a plain program's by a relative error of at most 0.0001.
Values sent between devices are 32-bit elements; how exact they have to be, the bound alone decides.
A program may use at most 64 MiB of HBM per device.

v0:
```python
import math
import jax
import jax.numpy as jnp
from jax import lax
from jax.sharding import PartitionSpec as P

STEPS = 3


def per_device(theta, counts, pair_source, pair_target, left_ops, right_ops):
    op_count = lax.axis_size("op")
    op_place = lax.axis_index("op")
    sec_place = lax.axis_index("sec")
    sec_local = theta.shape[0]
    row_count = theta.shape[1]
    order_size = theta.shape[2]
    pairs_local = left_ops.shape[0]
    group_blocks = pair_target.shape[0]
    sectors_all = sec_local * lax.axis_size("sec")
    factor = 0.5 / math.sqrt(group_blocks * pairs_local / sec_local)
    highest = lax.Precision.HIGHEST
    my_source = lax.dynamic_index_in_dim(pair_source, op_place, 0, keepdims=False)
    row_numbers = op_place * row_count + jnp.arange(row_count, dtype=jnp.int32)
    row_alive = row_numbers[None, :] < counts[:, None]
    column_alive = jnp.arange(order_size, dtype=jnp.int32)[None, :] < counts[:, None]
    live_mask = (row_alive[:, :, None] & column_alive[:, None, :]).astype(jnp.float32)
    target_hot = (pair_target[None, :] == jnp.arange(sectors_all, dtype=jnp.int32)[:, None]).astype(
        jnp.float32
    )

    def hamiltonian(iterate):
        gathered = lax.all_gather(iterate, "op", axis=1, tiled=True)
        chosen = lax.dynamic_index_in_dim(gathered, my_source, 0, keepdims=False)
        left_product = jnp.einsum("pmr,rn->pmn", left_ops, chosen, precision=highest)
        block_term = jnp.einsum("pmk,pnk->mn", left_product, right_ops, precision=highest)
        split_rows = block_term.reshape(op_count, row_count, order_size)
        block_rows = lax.all_to_all(split_rows, "op", split_axis=0, concat_axis=0, tiled=True)
        flat_rows = block_rows.reshape(group_blocks, row_count * order_size)
        sector_sums = jnp.dot(
            target_hot, flat_rows, precision=highest, preferred_element_type=jnp.float32
        )
        sector_sums = sector_sums.reshape(sectors_all, row_count, order_size)
        whole_sums = lax.psum(sector_sums, "sec")
        own_sums = lax.dynamic_slice_in_dim(whole_sums, sec_place * sec_local, sec_local, 0)
        return factor * own_sums * live_mask

    previous = theta * live_mask
    current = hamiltonian(previous)
    for step_number in range(STEPS - 1):
        following = 2.0 * hamiltonian(current) - previous
        previous, current = (current, following)
    return (current, previous)


def solution(mesh):
    in_specs = (
        P("sec", "op", None),
        P("sec"),
        P("sec"),
        P("sec"),
        P(("sec", "op"), None, None),
        P(("sec", "op"), None, None),
    )
    out_specs = (P("sec", "op", None), P("sec", "op", None))
    return jax.shard_map(
        per_device, mesh=mesh, in_specs=in_specs, out_specs=out_specs, check_vma=False
    )
```

profile of v0, /device:TPU:1, one launch (start us, length us, event | category | flops | bytes accessed | tf_op | source)
XLA Modules:
  0.0 675.0 jit_solution(8471230393268469698)
XLA Ops:
  7.2 0.0 all-gather.4.cloned.1.call-start
  7.2 0.7 iota_compare_fusion.1
  8.0 0.7 broadcast_compare_fusion
  8.7 1.7 and_select_fusion.3
  10.4 0.0 all-gather.4.cloned.1.call-update
  10.4 0.0 all-reduce.4.cloned.1.call-start
  10.5 1.2 dynamic_slice.23
  13.7 50.3 %all-gather.4.cloned.1.call-done = f32[2,512,512]{2,0,1:T(2,128)} async-done(((f32[2,32,512]{2,0,1:T(2,128)}), f32[2,512,512]{2,0,1:T(2,128)}) %all-gather.4.cloned.1.call-update) | async-done | bytes 2097168 | tf_op jit(solution)/shard_map/all_gather | solution.py:32
  63.9 2.5 constant_dynamic-slice_fusion.2
  66.4 1.3 copy.18
  67.8 0.0 copy-start
  67.8 10.3 %fusion.19 = f32[512,4,512]{2,0,1:T(8,128)S(1)} fusion(f32[4,512,512]{2,1,0:T(8,128)} %param.10, f32[1,512,512]{1,2,0:T(8,128)S(1)} %copy.18), kind=kOutput, calls=%fused_computation.19 | convolution fusion | flops 6442450944 | bytes 9437184 | tf_op jit(solution)/shard_map/pmr,rn->pmn/dot_general | solution.py:34
  78.1 13.9 %fusion.4 = f32[512,512,1]{1,0,2:T(8,128)S(1)} fusion(f32[4,512,512]{2,1,0:T(8,128)S(1)} %copy-done, f32[512,4,512]{2,0,1:T(8,128)S(1)} %fusion.19), kind=kOutput, calls=%fused_computation.4 | convolution fusion | flops 6442450944 | bytes 9437184 | tf_op jit(solution)/shard_map/pmk,pnk->mn/dot_general | solution.py:35
  92.0 19.3 %all_to_all.15 = f32[16,32,512]{2,1,0:T(8,128)S(1)} all-to-all(f32[16,32,512]{2,1,0:T(8,128)S(1)} %bitcast.75), channel_id=1, replica_groups=mesh['sec'=16,'op'=16] {'op'}, dimensions={0} | all-to-all | bytes 2097152 | tf_op jit(solution)/shard_map/all_to_all | solution.py:37
  111.3 2.9 fusion.12
  114.2 0.0 all-reduce.4.cloned.1.call-update
  114.2 0.0 all-gather.6.cloned.1.call-start
  114.2 115.1 %all-reduce.4.cloned.1.call-done = f32[32,32,512]{2,0,1:T(8,128)} async-done(((f32[32,32,512]{2,0,1:T(8,128)}), f32[32,32,512]{2,0,1:T(8,128)}) %all-reduce.4.cloned.1.call-update) | async-done | bytes 2097168 | tf_op jit(solution)/shard_map/psum | solution.py:43
  229.4 1.8 and_select_fusion.2
  231.2 0.0 all-gather.6.cloned.1.call-update
  231.3 0.0 all-reduce.6.cloned.1.call-start
  231.3 50.7 %all-gather.6.cloned.1.call-done = f32[2,512,512]{2,0,1:T(2,128)} async-done(((f32[2,32,512]{2,0,1:T(2,128)}), f32[2,512,512]{2,0,1:T(2,128)}) %all-gather.6.cloned.1.call-update) | async-done | bytes 2097168 | tf_op jit(solution)/shard_map/all_gather | solution.py:32
  282.0 2.5 constant_dynamic-slice_fusion.1
  284.5 1.3 copy.21
  285.8 10.3 %fusion.17 = f32[512,4,512]{2,0,1:T(8,128)S(1)} fusion(f32[4,512,512]{2,1,0:T(8,128)} %param.10, f32[1,512,512]{1,2,0:T(8,128)S(1)} %copy.21), kind=kOutput, calls=%fused_computation.17 | convolution fusion | flops 6442450944 | bytes 9437184 | tf_op jit(solution)/shard_map/pmr,rn->pmn/dot_general | solution.py:34
  296.1 13.7 %fusion.2 = f32[512,512,1]{1,0,2:T(8,128)S(1)} fusion(f32[4,512,512]{2,1,0:T(8,128)S(1)} %copy-done.1, f32[512,4,512]{2,0,1:T(8,128)S(1)} %fusion.17), kind=kOutput, calls=%fused_computation.2 | convolution fusion | flops 6442450944 | bytes 9437184 | tf_op jit(solution)/shard_map/pmk,pnk->mn/dot_general | solution.py:35
  309.8 0.0 copy-start.4
  309.9 19.4 %all_to_all.16 = f32[16,32,512]{2,1,0:T(8,128)S(1)} all-to-all(f32[16,32,512]{2,1,0:T(8,128)S(1)} %bitcast.76), channel_id=1, replica_groups=mesh['sec'=16,'op'=16] {'op'}, dimensions={0} | all-to-all | bytes 2097152 | tf_op jit(solution)/shard_map/all_to_all | solution.py:37
  329.2 2.9 fusion.9
  332.1 0.0 all-reduce.6.cloned.1.call-update
  332.2 0.0 all-gather.8.cloned.1.call-start
  332.2 115.3 %all-reduce.6.cloned.1.call-done = f32[32,32,512]{2,0,1:T(8,128)} async-done(((f32[32,32,512]{2,0,1:T(8,128)}), f32[32,32,512]{2,0,1:T(8,128)}) %all-reduce.6.cloned.1.call-update) | async-done | bytes 2097168 | tf_op jit(solution)/shard_map/psum | solution.py:43
  447.5 1.9 fusion.22
  449.5 0.0 all-gather.8.cloned.1.call-update
  449.5 0.0 all-reduce.8.cloned.1.call-start
  449.5 50.4 %all-gather.8.cloned.1.call-done = f32[2,512,512]{2,0,1:T(2,128)} async-done(((f32[2,32,512]{2,0,1:T(2,128)}), f32[2,512,512]{2,0,1:T(2,128)}) %all-gather.8.cloned.1.call-update) | async-done | bytes 2097168 | tf_op jit(solution)/shard_map/all_gather | solution.py:32
  500.0 2.5 constant_dynamic-slice_fusion
  502.5 1.3 copy.24
  503.8 0.0 copy-start.2
  503.8 10.3 %fusion.15 = f32[512,4,512]{2,0,1:T(8,128)S(1)} fusion(f32[4,512,512]{2,1,0:T(8,128)} %param.10, f32[1,512,512]{1,2,0:T(8,128)S(1)} %copy.24), kind=kOutput, calls=%fused_computation.15 | convolution fusion | flops 6442450944 | bytes 9437184 | tf_op jit(solution)/shard_map/pmr,rn->pmn/dot_general | solution.py:34
  514.1 13.8 %fusion = f32[512,512,1]{1,0,2:T(8,128)S(1)} fusion(f32[4,512,512]{2,1,0:T(8,128)S(1)} %copy-done.2, f32[512,4,512]{2,0,1:T(8,128)S(1)} %fusion.15), kind=kOutput, calls=%fused_computation | convolution fusion | flops 6442450944 | bytes 9437184 | tf_op jit(solution)/shard_map/pmk,pnk->mn/dot_general | solution.py:35
  528.0 19.4 %all_to_all.17 = f32[16,32,512]{2,1,0:T(8,128)S(1)} all-to-all(f32[16,32,512]{2,1,0:T(8,128)S(1)} %bitcast.77), channel_id=1, replica_groups=mesh['sec'=16,'op'=16] {'op'}, dimensions={0} | all-to-all | bytes 2097152 | tf_op jit(solution)/shard_map/all_to_all | solution.py:37
  547.4 2.9 fusion.6
  550.3 0.0 all-reduce.8.cloned.1.call-update
  550.3 0.7 copy.28
  551.0 114.5 %all-reduce.8.cloned.1.call-done = f32[32,32,512]{2,0,1:T(8,128)} async-done(((f32[32,32,512]{2,0,1:T(8,128)}), f32[32,32,512]{2,0,1:T(8,128)}) %all-reduce.8.cloned.1.call-update) | async-done | bytes 2097168 | tf_op jit(solution)/shard_map/psum | solution.py:43
  665.5 1.4 fusion.24
  666.9 0.7 copy.27
  (10 shorter events, 0.0 us)
Async XLA Ops:
  7.2 56.8 %all-gather.4.cloned.1.call-start = ((), (), s32[]{:S(2)}) async-start(), calls=%async_computation.3 | async-start | bytes 2228224 | tf_op jit(solution)/shard_map/all_gather | solution.py:32
  10.4 219.0 %all-reduce.4.cloned.1.call-start = ((), (), s32[]{:S(2)}) async-start(), calls=%async_computation.4 | async-start | bytes 4194304 | tf_op jit(solution)/shard_map/psum | solution.py:43
  67.8 10.3 %copy-start = (f32[4,512,512]{2,1,0:T(8,128)S(1)}, f32[4,512,512]{2,1,0:T(8,128)}, u32[]{:S(2)}) copy-start(f32[4,512,512]{2,1,0:T(8,128)} %param.11) | copy-start | bytes 12582916
  78.1 33.2 %copy-start.5 = (s32[16]{0:T(128)S(1)}, s32[16]{0:T(128)}, u32[]{:S(2)}) copy-start(s32[16]{0:T(128)} %param.9) | copy-start | bytes 196
  114.2 167.8 %all-gather.6.cloned.1.call-start = ((), (), s32[]{:S(2)}) async-start(), calls=%async_computation.5 | async-start | bytes 2228224 | tf_op jit(solution)/shard_map/all_gather | solution.py:32
  231.3 216.3 %all-reduce.6.cloned.1.call-start = ((), (), s32[]{:S(2)}) async-start(), calls=%async_computation.6 | async-start | bytes 4194304 | tf_op jit(solution)/shard_map/psum | solution.py:43
  285.8 10.3 %copy-start.1 = (f32[4,512,512]{2,1,0:T(8,128)S(1)}, f32[4,512,512]{2,1,0:T(8,128)}, u32[]{:S(2)}) copy-start(f32[4,512,512]{2,1,0:T(8,128)} %param.11) | copy-start | bytes 12582916
  309.8 137.7 %copy-start.4 = (f32[2,32,512]{2,1,0:T(8,128)S(1)}, f32[2,32,512]{2,1,0:T(8,128)}, u32[]{:S(2)}) copy-start(f32[2,32,512]{2,1,0:T(8,128)} %param.6) | copy-start | bytes 393220
  332.2 167.8 %all-gather.8.cloned.1.call-start = ((), (), s32[]{:S(2)}) async-start(), calls=%async_computation.7 | async-start | bytes 2228224 | tf_op jit(solution)/shard_map/all_gather | solution.py:32
  449.5 216.0 %all-reduce.8.cloned.1.call-start = ((), (), s32[]{:S(2)}) async-start(), calls=%async_computation.8 | async-start | bytes 4194304 | tf_op jit(solution)/shard_map/psum | solution.py:43
  503.8 10.4 %copy-start.2 = (f32[4,512,512]{2,1,0:T(8,128)S(1)}, f32[4,512,512]{2,1,0:T(8,128)}, u32[]{:S(2)}) copy-start(f32[4,512,512]{2,1,0:T(8,128)} %param.11) | copy-start | bytes 12582916
  528.0 22.3 %copy-start.3 = (f32[2,32,512]{2,0,1:T(2,128)S(1)}, f32[2,32,512]{2,0,1:T(2,128)}, u32[]{:S(2)}) copy-start(f32[2,32,512]{2,0,1:T(2,128)} %fusion.22) | copy-start | bytes 393220
Sparse Core Ops, SparseCore 0:
  11.0 52.8 all-gather.3
  114.3 115.0 all-reduce.3
  232.4 49.5 all-gather.5
  332.3 115.2 all-reduce.5
  450.4 49.5 all-gather.7
  550.4 115.0 all-reduce.7
where the time goes:
time: 680 us; the launch traced here: 675 us
  waiting for transfers between devices  496 us (73%)
  matrix products  81 us (12%)
  blocking collectives  58 us (9%)
  between operations  16.7 us (2%)
  local copies, waits for them, and re-layouts  14 us (2%)
  other arithmetic  8.39 us (1%)
    psum x3, waiting for transfers between devices, hamiltonian(): whole_sums = lax.psum(sector_sums, 'sec')  345 us
    all_gather x3, waiting for transfers between devices, hamiltonian(): gathered = lax.all_gather(iterate, 'op', axis=1, tiled=True)  151 us
    all_to_all x3, blocking collectives, hamiltonian(): lax.all_to_all(split_rows, 'op', split_axis=0, concat_axis=0, tiled=True)  58 us
    dot_general x3, matrix products, hamiltonian(): jnp.einsum('pmk,pnk->mn', left_product, right_ops, precision=highest)  41.5 us
    dot_general x3, matrix products, hamiltonian(): jnp.einsum('pmr,rn->pmn', left_ops, chosen, precision=highest)  30.9 us
  transfers between devices with their start and end apart: 6, of which 6 were waited for; matrix products, arithmetic and copies ran while one was open for 0% of the time, Pallas kernels for 0%

commit v1 on v0

--- a/solution.py
+++ b/solution.py
@@ -29,7 +29,9 @@
     )
 
     def hamiltonian(iterate):
-        gathered = lax.all_gather(iterate, "op", axis=1, tiled=True)
+        gathered = jnp.concatenate(
+            lax.all_to_all(jnp.stack([iterate] * lax.axis_size("op")), "op", 0, 0), axis=1
+        )
         chosen = lax.dynamic_index_in_dim(gathered, my_source, 0, keepdims=False)
         left_product = jnp.einsum("pmr,rn->pmn", left_ops, chosen, precision=highest)
         block_term = jnp.einsum("pmk,pnk->mn", left_product, right_ops, precision=highest)

time: 680 us -> 641 us (0.943)
  waiting for transfers between devices: 496 us -> 373 us
  blocking collectives: 58 us -> 121 us
  matrix products: 81 us -> 101 us
  local copies, waits for them, and re-layouts: 14 us -> 6.14 us
  starting transfers between devices: 0.25 us -> 7.71 us
    all_gather x3 -> x0, waiting for transfers between devices: 151 us -> none  [hamiltonian(): gathered = lax.all_gather(iterate, 'op', axis=1, tiled=True)]
    all_to_all x0 -> x2, blocking collectives: none -> 66.6 us  [hamiltonian(): lax.all_to_all(jnp.stack([iterate] * lax.axis_size('op')), 'op', 0, 0)]
    all_to_all x0 -> x1, waiting for transfers between devices: none -> 25.3 us  [hamiltonian(): lax.all_to_all(jnp.stack([iterate] * lax.axis_size('op')), 'op', 0, 0)]
    dynamic_slice x6 -> x0, local copies, waits for them, and re-layouts: 11.4 us -> none  [hamiltonian(): chosen = lax.dynamic_index_in_dim(gathered, my_source, 0, keepdims=False)]
    dot_general x3, matrix products: 41.5 us -> 51.5 us  [hamiltonian(): jnp.einsum('pmk,pnk->mn', left_product, right_ops, precision=highest)]
    dot_general x3, matrix products: 30.9 us -> 40.7 us  [hamiltonian(): jnp.einsum('pmr,rn->pmn', left_ops, chosen, precision=highest)]
    all_to_all x0 -> x1, starting transfers between devices: none -> 7.58 us  [hamiltonian(): lax.all_to_all(jnp.stack([iterate] * lax.axis_size('op')), 'op', 0, 0)]
  transfers between devices with their start and end apart: 6 -> 4, of which waited for: 6 -> 4; matrix products, arithmetic and copies ran while one was open for 0% -> 0% of each run, Pallas kernels for 0% -> 0%
where the time goes in v1:
time: 641 us; the launch traced here: 631 us
  waiting for transfers between devices  373 us (58%)
  blocking collectives  121 us (19%)
  matrix products  101 us (16%)
  between operations  16.4 us (3%)
  starting transfers between devices  7.71 us (1%)
  other arithmetic  6.44 us (1%)
    psum x3, waiting for transfers between devices, hamiltonian(): whole_sums = lax.psum(sector_sums, 'sec')  347 us
    all_to_all x2, blocking collectives, hamiltonian(): lax.all_to_all(jnp.stack([iterate] * lax.axis_size('op')), 'op', 0, 0)  66.6 us
    all_to_all x3, blocking collectives, hamiltonian(): lax.all_to_all(split_rows, 'op', split_axis=0, concat_axis=0, tiled=True)  54.4 us
    dot_general x3, matrix products, hamiltonian(): jnp.einsum('pmk,pnk->mn', left_product, right_ops, precision=highest)  51.5 us
    dot_general x3, matrix products, hamiltonian(): jnp.einsum('pmr,rn->pmn', left_ops, chosen, precision=highest)  40.7 us
    all_to_all x1, waiting for transfers between devices, hamiltonian(): lax.all_to_all(jnp.stack([iterate] * lax.axis_size('op')), 'op', 0, 0)  25.3 us
  transfers between devices with their start and end apart: 4, of which 4 were waited for; matrix products, arithmetic and copies ran while one was open for 0% of the time, Pallas kernels for 0%

profile of v1, /device:TPU:1, one launch (start us, length us, event | category | flops | bytes accessed | tf_op | source)
XLA Modules:
  0.0 631.1 jit_solution(7749390649929183729)
XLA Ops:
  7.2 0.0 copy-start.9
  7.2 0.7 iota_compare_fusion.1
  7.9 0.7 broadcast_compare_fusion
  8.6 1.1 and_select_fusion.3
  9.8 1.6 stack.6
  11.4 7.6 %all-to-all-start = ((f32[16,2,32,512]{3,2,1,0:T(8,128)}), f32[16,2,32,512]{3,2,1,0:T(8,128)S(1)}, u32[]{:S(2)}, u32[]{:S(2)}) async-start(f32[16,2,32,512]{3,2,1,0:T(8,128)} %stack.6), calls=%async_computation | async-start | bytes 4194304 | tf_op jit(solution)/shard_map/all_to_all | solution.py:33
  19.0 0.0 all-reduce.4.cloned.1.call-start
  19.0 0.6 dynamic_slice.23
  21.6 25.3 %all-to-all-done = f32[16,2,32,512]{3,2,1,0:T(8,128)S(1)} async-done(((f32[16,2,32,512]{3,2,1,0:T(8,128)}), f32[16,2,32,512]{3,2,1,0:T(8,128)S(1)}, u32[]{:S(2)}, u32[]{:S(2)}) %all-to-all-start) | async-done | bytes 2097184 | tf_op jit(solution)/shard_map/all_to_all | solution.py:33
  46.8 0.2 copy.25
  47.0 2.0 copy-done
  49.0 13.5 %fusion.19 = f32[512,4,512]{2,0,1:T(8,128)S(1)} fusion(f32[4,512,512]{2,1,0:T(8,128)S(1)} %copy-done, f32[2,512,512]{2,1,0:T(8,128)S(1)} %bitcast.88, s32[]{:T(128)S(6)} %select_n.16), kind=kOutput, calls=%fused_computation.19 | convolution fusion | flops 6442450944 | bytes 9437188 | tf_op jit(solution)/shard_map/pmr,rn->pmn/dot_general | solution.py:36
  62.6 0.0 copy-start.8
  62.6 24.6 %fusion.4 = f32[512,512,1]{1,0,2:T(8,128)S(1)} fusion(f32[4,512,512]{2,1,0:T(8,128)S(1)} %copy-done.3, f32[512,4,512]{2,0,1:T(8,128)S(1)} %fusion.19), kind=kOutput, calls=%fused_computation.4 | convolution fusion | flops 6442450944 | bytes 9437184 | tf_op jit(solution)/shard_map/pmk,pnk->mn/dot_general | solution.py:37
  87.2 16.9 %all_to_all.30 = f32[16,32,512]{2,1,0:T(8,128)S(1)} all-to-all(f32[16,32,512]{2,1,0:T(8,128)S(1)} %bitcast.90), channel_id=1, replica_groups=mesh['sec'=16,'op'=16] {'op'}, dimensions={0} | all-to-all | bytes 2097152 | tf_op jit(solution)/shard_map/all_to_all | solution.py:39
  104.1 2.9 fusion.12
  107.0 0.0 all-reduce.4.cloned.1.call-update
  107.0 0.0 all-reduce.6.cloned.1.call-start
  107.1 118.2 %all-reduce.4.cloned.1.call-done = f32[32,32,512]{2,0,1:T(8,128)} async-done(((f32[32,32,512]{2,0,1:T(8,128)}), f32[32,32,512]{2,0,1:T(8,128)}) %all-reduce.4.cloned.1.call-update) | async-done | bytes 2097168 | tf_op jit(solution)/shard_map/psum | solution.py:45
  225.2 1.2 and_select_fusion.2
  226.5 0.2 stack.7
  226.7 0.0 copy-start.1
  226.7 33.3 %all_to_all.31 = f32[16,2,32,512]{3,2,1,0:T(8,128)S(1)} all-to-all(f32[16,2,32,512]{3,2,1,0:T(8,128)S(1)} %stack.7), channel_id=1, replica_groups=mesh['sec'=16,'op'=16] {'op'}, dimensions={0} | all-to-all | bytes 4194304 | tf_op jit(solution)/shard_map/all_to_all | solution.py:33
  260.0 0.2 copy.30
  260.3 0.0 copy-start.4
  260.3 13.7 %fusion.17 = f32[512,4,512]{2,0,1:T(8,128)S(1)} fusion(f32[4,512,512]{2,1,0:T(8,128)S(1)} %copy-done.1, f32[2,512,512]{2,1,0:T(8,128)S(1)} %bitcast.89, s32[]{:T(128)S(6)} %select_n.16), kind=kOutput, calls=%fused_computation.17 | convolution fusion | flops 6442450944 | bytes 9437188 | tf_op jit(solution)/shard_map/pmr,rn->pmn/dot_general | solution.py:36
  274.0 13.4 %fusion.2 = f32[512,512,1]{1,0,2:T(8,128)S(1)} fusion(f32[4,512,512]{2,1,0:T(8,128)S(1)} %copy-done.4, f32[512,4,512]{2,0,1:T(8,128)S(1)} %fusion.17), kind=kOutput, calls=%fused_computation.2 | convolution fusion | flops 6442450944 | bytes 9437184 | tf_op jit(solution)/shard_map/pmk,pnk->mn/dot_general | solution.py:37
  287.4 0.0 copy-start.7
  287.4 18.8 %all_to_all.32 = f32[16,32,512]{2,1,0:T(8,128)S(1)} all-to-all(f32[16,32,512]{2,1,0:T(8,128)S(1)} %bitcast.91), channel_id=1, replica_groups=mesh['sec'=16,'op'=16] {'op'}, dimensions={0} | all-to-all | bytes 2097152 | tf_op jit(solution)/shard_map/all_to_all | solution.py:39
  306.2 2.9 fusion.9
  309.1 0.0 all-reduce.6.cloned.1.call-update
  309.1 0.0 all-reduce.8.cloned.1.call-start
  309.2 114.6 %all-reduce.6.cloned.1.call-done = f32[32,32,512]{2,0,1:T(8,128)} async-done(((f32[32,32,512]{2,0,1:T(8,128)}), f32[32,32,512]{2,0,1:T(8,128)}) %all-reduce.6.cloned.1.call-update) | async-done | bytes 2097168 | tf_op jit(solution)/shard_map/psum | solution.py:45
  423.7 1.3 fusion.25
  425.0 0.0 copy-start.6
  425.1 0.3 stack.8
  425.3 0.0 copy-start.2
  425.3 33.3 %all_to_all.33 = f32[16,2,32,512]{3,2,1,0:T(8,128)S(1)} all-to-all(f32[16,2,32,512]{3,2,1,0:T(8,128)S(1)} %stack.8), channel_id=1, replica_groups=mesh['sec'=16,'op'=16] {'op'}, dimensions={0} | all-to-all | bytes 4194304 | tf_op jit(solution)/shard_map/all_to_all | solution.py:33
  458.6 0.2 copy.35
  458.9 0.0 copy-start.5
  458.9 13.5 %fusion.15 = f32[512,4,512]{2,0,1:T(8,128)S(1)} fusion(f32[4,512,512]{2,1,0:T(8,128)S(1)} %copy-done.2, f32[2,512,512]{2,1,0:T(8,128)S(1)} %bitcast.87, s32[]{:T(128)S(6)} %select_n.16), kind=kOutput, calls=%fused_computation.15 | convolution fusion | flops 6442450944 | bytes 9437188 | tf_op jit(solution)/shard_map/pmr,rn->pmn/dot_general | solution.py:36
  472.4 13.5 %fusion = f32[512,512,1]{1,0,2:T(8,128)S(1)} fusion(f32[4,512,512]{2,1,0:T(8,128)S(1)} %copy-done.5, f32[512,4,512]{2,0,1:T(8,128)S(1)} %fusion.15), kind=kOutput, calls=%fused_computation | convolution fusion | flops 6442450944 | bytes 9437184 | tf_op jit(solution)/shard_map/pmk,pnk->mn/dot_general | solution.py:37
  485.9 18.7 %all_to_all.34 = f32[16,32,512]{2,1,0:T(8,128)S(1)} all-to-all(f32[16,32,512]{2,1,0:T(8,128)S(1)} %bitcast.92), channel_id=1, replica_groups=mesh['sec'=16,'op'=16] {'op'}, dimensions={0} | all-to-all | bytes 2097152 | tf_op jit(solution)/shard_map/all_to_all | solution.py:39
  504.6 2.9 fusion.6
  507.4 0.0 all-reduce.8.cloned.1.call-update
  507.5 114.6 %all-reduce.8.cloned.1.call-done = f32[32,32,512]{2,0,1:T(8,128)} async-done(((f32[32,32,512]{2,0,1:T(8,128)}), f32[32,32,512]{2,0,1:T(8,128)}) %all-reduce.8.cloned.1.call-update) | async-done | bytes 2097168 | tf_op jit(solution)/shard_map/psum | solution.py:45
  622.1 1.4 fusion.27
  623.5 0.7 copy.39
  (15 shorter events, 0.1 us)
Async XLA Ops:
  7.2 11.8 %copy-start.9 = (s32[16]{0:T(128)S(1)}, s32[16]{0:T(128)}, u32[]{:S(2)}) copy-start(s32[16]{0:T(128)} %param.8) | copy-start | bytes 196
  11.4 35.5 %all-to-all-start = ((f32[16,2,32,512]{3,2,1,0:T(8,128)}), f32[16,2,32,512]{3,2,1,0:T(8,128)S(1)}, u32[]{:S(2)}, u32[]{:S(2)}) async-start(f32[16,2,32,512]{3,2,1,0:T(8,128)} %stack.6), calls=%async_computation | async-start | bytes 4194304 | tf_op jit(solution)/shard_map/all_to_all | solution.py:33
  19.0 206.3 %all-reduce.4.cloned.1.call-start = ((), (), s32[]{:S(2)}) async-start(), calls=%async_computation.6 | async-start | bytes 4194304 | tf_op jit(solution)/shard_map/psum | solution.py:45
  46.8 2.2 copy-start
  49.0 13.5 %copy-start.3 = (f32[4,512,512]{2,1,0:T(8,128)S(1)}, f32[4,512,512]{2,1,0:T(8,128)}, u32[]{:S(2)}) copy-start(f32[4,512,512]{2,1,0:T(8,128)} %param.11) | copy-start | bytes 12582916
  62.6 41.5 %copy-start.8 = (s32[16]{0:T(128)S(1)}, s32[16]{0:T(128)}, u32[]{:S(2)}) copy-start(s32[16]{0:T(128)} %param.9) | copy-start | bytes 196
  107.0 316.7 %all-reduce.6.cloned.1.call-start = ((), (), s32[]{:S(2)}) async-start(), calls=%async_computation.7 | async-start | bytes 4194304 | tf_op jit(solution)/shard_map/psum | solution.py:45
  226.7 33.6 %copy-start.1 = (f32[4,512,512]{2,1,0:T(8,128)S(1)}, f32[4,512,512]{2,1,0:T(8,128)}, u32[]{:S(2)}) copy-start(f32[4,512,512]{2,1,0:T(8,128)} %param.10) | copy-start | bytes 12582916
  260.3 13.7 %copy-start.4 = (f32[4,512,512]{2,1,0:T(8,128)S(1)}, f32[4,512,512]{2,1,0:T(8,128)}, u32[]{:S(2)}) copy-start(f32[4,512,512]{2,1,0:T(8,128)} %param.11) | copy-start | bytes 12582916
  287.4 136.3 %copy-start.7 = (f32[2,32,512]{2,1,0:T(8,128)S(1)}, f32[2,32,512]{2,1,0:T(8,128)}, u32[]{:S(2)}) copy-start(f32[2,32,512]{2,1,0:T(8,128)} %param.6) | copy-start | bytes 393220
  309.1 313.0 %all-reduce.8.cloned.1.call-start = ((), (), s32[]{:S(2)}) async-start(), calls=%async_computation.8 | async-start | bytes 4194304 | tf_op jit(solution)/shard_map/psum | solution.py:45
  425.0 33.8 %copy-start.6 = (f32[2,32,512]{2,1,0:T(8,128)}, f32[2,32,512]{2,1,0:T(8,128)S(1)}, u32[]{:S(2)}) copy-start(f32[2,32,512]{2,1,0:T(8,128)S(1)} %copy.34) | copy-start | bytes 393220
  425.3 33.6 %copy-start.2 = (f32[4,512,512]{2,1,0:T(8,128)S(1)}, f32[4,512,512]{2,1,0:T(8,128)}, u32[]{:S(2)}) copy-start(f32[4,512,512]{2,1,0:T(8,128)} %param.10) | copy-start | bytes 12582916
  458.9 13.5 %copy-start.5 = (f32[4,512,512]{2,1,0:T(8,128)S(1)}, f32[4,512,512]{2,1,0:T(8,128)}, u32[]{:S(2)}) copy-start(f32[4,512,512]{2,1,0:T(8,128)} %param.11) | copy-start | bytes 12582916
Sparse Core Ops, SparseCore 0:
  107.1 118.0 all-reduce.3
  309.2 114.4 all-reduce.5
  507.6 114.4 all-reduce.7
